TPU v7x, 32 devices: a whole 2x2x4 slice. The times are simulated.
32 devices in a mesh: groups: 1, row: 16 (over z, y, core), col: 2 (over x), freq: 1.
Axes of the slice: x: 2, y: 2, z: 4, core: 2. Of those that a mesh axis runs over, the one named last changes fastest.
Arguments:
- traces: bfloat16 [256, 96000], P(('groups', 'row', 'col')), may hold values from -6 to 6
- slot_channel: int32 [256], P(('groups', 'row', 'col')), may hold values from 0 to 255, as said below
- usable_blocks: int32 [32], P(('groups', 'row', 'col')), may hold values 0 or 1
Outputs:
- correlation: float32 [65, 256, 256], P(None, ('groups', 'row'), ('col', 'freq'))
Inputs may be any that keep to these rules, and one draw needn't show every extreme that they name: `slot_channel`: every channel is recorded in exactly one slot, and the 16 slots of each aligned block of 16 slots hold the 16 fiber channels of that same block.
All inputs are finite; a program needn't handle non-finite values. No bound on the sum of `usable_blocks` on one device may be relied on, other than what follows from the above.
Results may differ from a plain program's by a relative error of at most 0.0054.
Values may be sent and summed in bfloat16 or wider, within the bound.
A program may use at most 64 MiB of HBM per device.

v0:
```python
import math

import jax
import jax.numpy as jnp
from jax import lax
from jax.sharding import PartitionSpec as P

SEG = 300
FREQS = 64
MAXLAG = 32


water_level = 0.5
corr_gain = 3.0


def lag_weights(bin_numbers, segment_total):
    lag_steps = jnp.arange(2 * MAXLAG + 1, dtype=jnp.int32) - MAXLAG
    lag_turns = lag_steps[:, None] * bin_numbers[None, :] % SEG
    lag_angles = 2.0 * math.pi / SEG * lag_turns.astype(jnp.float32)
    norm_gain = corr_gain / math.sqrt(segment_total * FREQS)
    return jnp.stack(
        [norm_gain * jnp.cos(lag_angles), -norm_gain * jnp.sin(lag_angles)], axis=-1
    ).astype(jnp.bfloat16)


def body(traces, slot_channel, usable_blocks):
    own_count = traces.shape[0]
    segment_total = traces.shape[1] // SEG
    local_bins = FREQS // lax.axis_size("freq")
    freq_index = lax.axis_index("freq")
    row_index = lax.axis_index("row")
    col_index = lax.axis_index("col")
    samples = jnp.arange(SEG, dtype=jnp.int32)
    taper = 0.5 - 0.5 * jnp.cos(2.0 * math.pi / SEG * samples.astype(jnp.float32))
    bin_numbers = 1 + freq_index * local_bins + jnp.arange(local_bins, dtype=jnp.int32)
    turns = samples[:, None] * bin_numbers[None, :] % SEG
    angles = 2.0 * math.pi / SEG * turns.astype(jnp.float32)
    dft_table = jnp.concatenate(
        [taper[:, None] * jnp.cos(angles), -taper[:, None] * jnp.sin(angles)], axis=1
    ).astype(jnp.bfloat16)
    pieces = traces.reshape(own_count, segment_total, SEG)
    coefficients = jnp.einsum("csn,nq->csq", pieces, dft_table, preferred_element_type=jnp.float32)
    windowed = pieces.astype(jnp.float32) * taper
    level = jnp.sqrt(SEG * (jnp.mean(windowed * windowed, axis=-1) + 1e-05))
    real_part = coefficients[..., :local_bins]
    imag_part = coefficients[..., local_bins:]
    divisor = (
        jnp.sqrt(real_part * real_part + imag_part * imag_part) + water_level * level[..., None]
    )
    white_real = jnp.transpose((real_part / divisor).astype(jnp.bfloat16), (0, 2, 1))
    white_imag = jnp.transpose((imag_part / divisor).astype(jnp.bfloat16), (0, 2, 1))
    own_spectra = jnp.concatenate([white_real, white_imag], axis=-1)
    block_spectra, block_slots, block_usable = (
        lax.all_gather(own_spectra, "col", axis=0, tiled=True),
        lax.all_gather(slot_channel, "col", axis=0, tiled=True),
        lax.all_gather(usable_blocks, "col", axis=0, tiled=True),
    )
    block_size = block_spectra.shape[0]
    positions = block_slots % block_size
    one_hot = (positions[None, :] == jnp.arange(block_size, dtype=jnp.int32)[:, None]).astype(
        jnp.bfloat16
    )
    ordered = jnp.einsum(
        "us,sfk->ufk", one_hot, block_spectra, preferred_element_type=jnp.float32
    ).astype(jnp.bfloat16)
    usable = jnp.repeat(block_usable, own_count, total_repeat_length=block_size).astype(
        jnp.bfloat16
    )
    ordered = ordered * usable[:, None, None]
    rotated = jnp.concatenate(
        [ordered[..., segment_total:], -ordered[..., :segment_total]], axis=-1
    )
    stacked_rows = jnp.concatenate([ordered, rotated], axis=0)
    quarter = lax.dynamic_slice_in_dim(ordered, col_index * own_count, own_count, 0)
    column_total = own_count * lax.axis_size("row")
    empty_sum = jnp.zeros((local_bins, 2 * block_size, column_total), jnp.float32)
    product = jnp.einsum(
        "afk,bfk->fab",
        stacked_rows,
        lax.all_gather(quarter, "row", axis=0, tiled=True),
        preferred_element_type=jnp.float32,
    )
    cross = lax.dynamic_update_slice_in_dim(empty_sum, product, jnp.int32(0), 2)
    stacked = cross.astype(jnp.bfloat16).reshape(local_bins, 2, block_size, column_total)
    lag_table = lag_weights(bin_numbers, segment_total)
    partial_lags = jnp.einsum(
        "lfp,fpab->lab", lag_table, stacked, preferred_element_type=jnp.float32
    )
    result = lax.psum_scatter(partial_lags, "freq", scatter_dimension=2, tiled=True)
    out_width = result.shape[2]
    columns = freq_index * out_width + jnp.arange(out_width, dtype=jnp.int32)
    column_block = columns // own_count
    column_place = col_index * own_count + columns % own_count
    row_place = jnp.arange(block_size, dtype=jnp.int32)
    same = (column_block[None, :] == row_index) & (row_place[:, None] == column_place[None, :])
    return jnp.where(same[None, :, :], jnp.float32(0.0), result)


def solution(mesh):
    in_specs = (
        P(("groups", "row", "col"), None),
        P(("groups", "row", "col")),
        P(("groups", "row", "col")),
    )
    out_specs = P(None, ("groups", "row"), ("col", "freq"))
    return jax.shard_map(body, mesh=mesh, in_specs=in_specs, out_specs=out_specs, check_vma=False)
```

profile of v0, /device:TPU:0, one launch (start us, length us, event | category | flops | bytes accessed | tf_op | source)
XLA Modules:
  0.0 153.8 jit_solution(13554173547557373578)
XLA Ops:
  6.5 0.0 all-gather.3.cloned.1.call-start
  6.6 3.7 %reshape.286 = bf16[768000]{0:T(1024)(128)(2,1)S(1)} reshape(bf16[8,96000]{1,0:T(8,128)(2,1)} %param.5) | data formatting | bytes 3072000
  10.3 5.1 %reshape.261 = bf16[8,320,300]{2,1,0:T(8,128)(2,1)S(1)} reshape(bf16[768000]{0:T(1024)(128)(2,1)S(1)} %reshape.286) | data formatting | bytes 3072000 | tf_op jit(solution)/shard_map/reshape | solution.py:42
  15.4 0.6 multiply_reduce_fusion
  16.1 0.7 multiply_convert_fusion.1
  16.8 0.8 convolution_bitcast_fusion
  17.5 0.8 fusion.12
  18.4 0.3 pad_maximum_fusion
  18.6 0.0 copy-start.2
  18.6 0.0 copy-start.1
  18.6 0.0 copy-start
  18.7 1.3 copy.13
  20.0 0.0 all-gather.3.cloned.1.call-update
  20.0 0.0 all-gather.5.cloned.1.call-start
  20.7 0.0 copy-done.2
  20.7 0.6 dynamic-slice.6
  21.9 0.0 copy-done.1
  21.9 0.2 dynamic-update-slice.3
  22.2 0.8 dynamic-update-slice.4
  22.9 5.2 %all-reduce.2 = (s32[2]{0:T(128)S(1)}, s32[16]{0:T(128)S(1)}) all-reduce(s32[2]{0:T(128)S(1)} %dynamic-update-slice.4, s32[16]{0:T(128)S(1)} %dynamic-update-slice.3), channel_id=1, replica_groups=mesh['groups'=1,'row'=16,'col'=2,'freq'=1] {'col'}, use_global_device_ids=true, to_apply=%add.1 | all-reduce | flops 18 | bytes 144
  28.1 0.6 fusion.41
  28.7 0.0 copy-done
  28.7 1.3 and_select_fusion
  30.0 17.1 %all-gather.3.cloned.1.call-done = bf16[16,64,640]{2,1,0:T(8,128)(2,1)} async-done(((bf16[8,64,640]{2,1,0:T(8,128)(2,1)}), bf16[16,64,640]{2,1,0:T(8,128)(2,1)}) %all-gather.3.cloned.1.call-update) | async-done | bytes 1310736 | tf_op jit(solution)/shard_map/all_gather | solution.py:55
  47.1 2.2 %fusion.6 = bf16[16,64,640]{2,0,1:T(8,128)(2,1)S(1)} fusion(bf16[16,64,640]{2,1,0:T(8,128)(2,1)} %all-gather.3.cloned.1.call-done, bf16[16]{0:T(256)(128)(2,1)S(1)} %get-tuple-element.32, s32[16]{0:T(128)S(1)} %get-tuple-element.31), kind=kOutput, calls=%fused_computation.8 | convolution fusion | flops 22282496 | bytes 2621536 | tf_op jit(solution)/shard_map/us,sfk->ufk/dot_general | solution.py:64
  49.3 0.9 constant_dynamic-slice_fusion
  50.2 0.0 all-gather.5.cloned.1.call-update
  50.3 0.2 multiply_convert_fusion.3
  50.5 0.3 fusion.40
  50.8 87.3 %all-gather.5.cloned.1.call-done = bf16[128,64,640]{2,0,1:T(8,128)(2,1)} async-done(((bf16[8,64,640]{2,0,1:T(8,128)(2,1)}), bf16[128,64,640]{2,0,1:T(8,128)(2,1)}) %all-gather.5.cloned.1.call-update) | async-done | bytes 10485776 | tf_op jit(solution)/shard_map/all_gather | solution.py:81
  138.2 7.5 %fusion.8 = bf16[64,32,128]{2,1,0:T(8,128)(2,1)S(1)} fusion(bf16[128,64,640]{2,0,1:T(8,128)(2,1)} %all-gather.5.cloned.1.call-done, bf16[16,64,320]{2,0,1:T(8,128)(2,1)S(1)} %get-tuple-element.22, bf16[16,64,320]{2,0,1:T(8,128)(2,1)S(1)} %get-tuple-element.21, bf16[16,64,640]{2,0,1:T(8,128)(2,1)S(1)} %fusion.6), kind=kOutput, calls=%fused_computation.15 | convolution fusion | flops 343670784 | bytes 13631488 | tf_op jit(solution)/shard_map/afk,bfk->fab/dot_general | solution.py:78
  145.7 0.3 fusion.11
  146.0 0.9 copy.16
  (9 shorter events, 0.1 us)
Async XLA Ops:
  6.5 40.6 %all-gather.3.cloned.1.call-start = ((), (), s32[]{:S(2)}) async-start(), calls=%async_computation | async-start | bytes 1966080 | tf_op jit(solution)/shard_map/all_gather | solution.py:55
  18.6 2.1 %copy-start.2 = (u32[32]{0:T(128)S(1)}, u32[32]{0:T(128)}, u32[]{:S(2)}) copy-start(u32[32]{0:T(128)} %constant.188) | copy-start | bytes 388
  18.6 3.3 %copy-start.1 = (s32[8]{0:T(128)S(1)}, s32[8]{0:T(128)}, u32[]{:S(2)}) copy-start(s32[8]{0:T(128)} %param.6) | copy-start | bytes 100
  18.6 10.1 %copy-start = (pred[16]{0:T(512)(128)(4,1)S(1)}, pred[16]{0:T(512)(128)(4,1)}, u32[]{:S(2)}) copy-start(pred[16]{0:T(512)(128)(4,1)} %constant.183) | copy-start | bytes 52
  20.0 118.2 %all-gather.5.cloned.1.call-start = ((), (), s32[]{:S(2)}) async-start(), calls=%async_computation.1 | async-start | bytes 11141120 | tf_op jit(solution)/shard_map/all_gather | solution.py:81
Sparse Core Ops, SparseCore 0:
  20.1 26.9 all-gather.2
  50.4 87.7 all-gather.4
where the time goes:
time: 154 us
  waiting for transfers between devices  104 us (68%)
  between operations  14.9 us (10%)
  local copies, waits for them, and re-layouts  14.1 us (9%)
  matrix products  10.8 us (7%)
  blocking collectives  5.19 us (3%)
  other arithmetic  4.27 us (3%)
    all_gather x1, waiting for transfers between devices, body(): lax.all_gather(quarter, 'row', axis=0, tiled=True)  87.3 us
    all_gather x1, waiting for transfers between devices, body(): lax.all_gather(own_spectra, 'col', axis=0, tiled=True)  17.1 us
    dot_general x1, matrix products, body(): jnp.einsum('afk,bfk->fab', stacked_rows, lax.all_gather(quarter, 'row', a...  7.52 us
    unnamed x12, local copies, waits for them, and re-layouts  5.3 us
    unnamed x1, blocking collectives  5.19 us
    reshape x1, local copies, waits for them, and re-layouts, body(): pieces = traces.reshape(own_count, segment_total, SEG)  5.13 us
  transfers between devices with their start and end apart: 2, of which 2 were waited for; matrix products, arithmetic and copies ran while one was open for 3% of the time, Pallas kernels for 0%

commit v1 on v0

--- a/solution.py
+++ b/solution.py
@@ -1,8 +1,12 @@
+import functools
 import math
 
 import jax
 import jax.numpy as jnp
+import numpy as np
 from jax import lax
+from jax.experimental import pallas as pl
+from jax.experimental.pallas import tpu as pltpu
 from jax.sharding import PartitionSpec as P
 
 SEG = 300
@@ -23,8 +27,7 @@
         [norm_gain * jnp.cos(lag_angles), -norm_gain * jnp.sin(lag_angles)], axis=-1
     ).astype(jnp.bfloat16)
 
-
-def body(traces, slot_channel, usable_blocks):
+def gather_body(traces, slot_channel, usable_blocks):
     own_count = traces.shape[0]
     segment_total = traces.shape[1] // SEG
     local_bins = FREQS // lax.axis_size("freq")
@@ -97,7 +100,264 @@
     return jnp.where(same[None, :, :], jnp.float32(0.0), result)
 
 
+LANES = 128
+SPAN = SEG * LANES // math.gcd(SEG, LANES)
+SPAN_SEGS = SPAN // SEG
+WIDE = -(-SEG // LANES) * LANES
+HALF = LANES // 2
+LAGS = 2 * MAXLAG + 1
+LAG_ROWS = -(-LAGS // 16) * 16
+
+
+def spectrum_table():
+    taper = 0.5 - 0.5 * np.cos(2.0 * np.pi / SEG * np.arange(SEG))
+    angles = 2.0 * np.pi / SEG * (np.arange(SEG)[:, None] * np.arange(1, FREQS + 1)[None, :] % SEG)
+    table = np.zeros((WIDE, 2 * FREQS), np.float32)
+    table[:SEG] = taper[:, None] * np.concatenate([np.cos(angles), -np.sin(angles)], axis=1)
+    wide_taper = np.zeros((8, WIDE), np.float32)
+    wide_taper[:, :SEG] = taper
+    return table.astype(jnp.bfloat16), wide_taper
+
+
+def lag_table(segment_total):
+    turns = (np.arange(LAGS) - MAXLAG)[:, None] * np.arange(1, FREQS + 1)[None, :] % SEG
+    angles = 2.0 * np.pi / SEG * turns
+    gain = corr_gain / math.sqrt(segment_total * FREQS)
+    table = np.zeros((LAG_ROWS, FREQS, 2), np.float32)
+    table[:LAGS, :, 0] = gain * np.cos(angles)
+    table[:LAGS, :, 1] = -gain * np.sin(angles)
+    return table.reshape(LAG_ROWS, 2 * FREQS).astype(jnp.bfloat16)
+
+
+def exchange_kernel(
+    rows, cols, traces, slots, usable, table, taper, lags, out,
+    samples, levels, white, spectra, send1, recv1, meta, recv_meta, send2, recv2, wide2, lagged,
+    s1, r1, sm, rm, s2, r2, own,
+):
+    f32, bf16 = jnp.float32, jnp.bfloat16
+    count = rows * cols
+    bins = FREQS // count
+    own_count = traces.shape[0]
+    block = own_count * cols
+    channels = own_count * count
+    group = bins * own_count
+    spans = traces.shape[1] // SPAN
+    row_index, col_index = lax.axis_index("row"), lax.axis_index("col")
+    me = row_index * cols + col_index
+
+    def peer(step):
+        other = lax.rem(me + step, count)
+        return other, {"row": other // cols, "col": lax.rem(other, cols)}
+
+    barrier = pltpu.get_barrier_semaphore()
+
+    def greet(step, carry):
+        pl.semaphore_signal(
+            barrier, inc=1, device_id=peer(step)[1], device_id_type=pl.DeviceIdType.MESH
+        )
+        return carry
+
+    lax.fori_loop(1, count, greet, 0)
+
+    sub = lax.broadcasted_iota(jnp.int32, (group, LANES), 0)
+    lane = lax.broadcasted_iota(jnp.int32, (group, LANES), 1)
+    place = jnp.zeros((group, LANES), jnp.int32)
+    for u in range(own_count):
+        place = jnp.where(sub % own_count == u, slots[u], place)
+    place = place + sub // own_count * channels
+    meta[...] = jnp.where(lane < HALF, place, usable[0])
+
+    def one_span(span, carry):
+        for s in range(0, SPAN_SEGS, 2):
+            pair = []
+            for q in (s, s + 1):
+                base = q * SEG // LANES * LANES
+                shift = q * SEG - base
+                width = -(-(shift + SEG) // LANES) * LANES
+                x = traces[:, pl.ds(pl.multiple_of(span * SPAN + base, LANES), width)].astype(f32)
+                if shift:
+                    x = pltpu.roll(x, width - shift, 1)
+                x = x[:, :WIDE]
+                windowed = x * taper[...]
+                power = jnp.sum(windowed * windowed, axis=1, keepdims=True)
+                level = water_level * jnp.sqrt(power + SEG * 1e-05)
+                levels[q * own_count : (q + 1) * own_count, :] = jnp.broadcast_to(
+                    level, (own_count, LANES)
+                )
+                pair.append(x)
+            samples[s * own_count : (s + 2) * own_count, :] = jnp.concatenate(pair, 0).astype(bf16)
+        y = jnp.dot(samples[...], table[...], preferred_element_type=f32)
+        square = y * y
+        magnitude = jnp.sqrt(square + pltpu.roll(square, FREQS, 1))
+        depth = SPAN_SEGS * own_count
+        white[pl.ds(pl.multiple_of(span * depth, depth), depth), :] = y / (magnitude + levels[...])
+        return carry
+
+    lax.fori_loop(0, spans, one_span, 0)
+
+    for u in range(own_count):
+        strip = pl.ds(u, FREQS, stride=own_count)
+        for t in range(2):
+            z = white[pl.ds(t * LANES * own_count + u, LANES, stride=own_count), :].T
+            spectra[t, strip, :] = z[:FREQS]
+            spectra[3 + t, strip, :] = z[FREQS:]
+        z = white[pl.ds(2 * LANES * own_count + u, HALF, stride=own_count), :]
+        z = jnp.concatenate([z, pltpu.roll(z, FREQS, 1)], 0).T
+        spectra[2, strip, :] = z[:FREQS]
+    for t in range(5):
+        send1[:, :, t * LANES : (t + 1) * LANES] = (
+            spectra[t].astype(bf16).reshape(count, group, LANES)
+        )
+
+    pl.semaphore_wait(barrier, count - 1)
+
+    def remote(src, dst, send_sem, recv_sem, target):
+        return pltpu.make_async_remote_copy(
+            src_ref=src, dst_ref=dst, send_sem=send_sem, recv_sem=recv_sem,
+            device_id=target, device_id_type=pl.DeviceIdType.MESH,
+        )
+
+    def first(step):
+        other, target = peer(step)
+        return (
+            remote(meta, recv_meta.at[me], sm.at[other], rm.at[me], target),
+            remote(send1.at[other], recv1.at[me], s1.at[other], r1.at[me], target),
+        )
+
+    def second(step):
+        other, target = peer(step)
+        return remote(send2.at[other], recv2.at[me], s2.at[other], r2.at[me], target)
+
+    def start_first(step, carry):
+        for copy in first(step):
+            copy.start()
+        return carry
+
+    lax.fori_loop(1, count, start_first, 0)
+    kept = pltpu.make_async_copy(send1.at[me], recv1.at[me], own.at[0])
+    kept.start()
+    recv_meta[me] = meta[...]
+    kept.wait()
+
+    def wait_first(step, carry):
+        other, target = peer(step)
+        remote(meta, recv_meta.at[other], sm.at[other], rm.at[other], target).wait()
+        remote(send1.at[other], recv1.at[other], s1.at[other], r1.at[other], target).wait()
+        return carry
+
+    lax.fori_loop(1, count, wait_first, 0)
+
+    known = recv_meta[...]
+    target_row = known.reshape(count * group, LANES).astype(f32).T[0:1, :]
+    good = known[:, :own_count, HALF : HALF + 1].reshape(channels, 1).astype(f32)
+    gathered = recv1[...].reshape(count * group, 5 * LANES)
+    lane_sign = jnp.where(lax.broadcasted_iota(jnp.int32, (1, LANES), 1) < HALF, 1.0, -1.0)
+    for b in range(bins):
+        row_number = lax.broadcasted_iota(jnp.int32, (channels, 1), 0) + b * channels
+        pick = jnp.where(row_number.astype(f32) == target_row, good, 0.0).astype(bf16)
+        ordered = jnp.dot(pick, gathered, preferred_element_type=f32)
+        mid = pltpu.roll(ordered[:, 2 * LANES : 3 * LANES], HALF, 1) * lane_sign
+        rotated = jnp.concatenate(
+            [ordered[:, 3 * LANES :], mid, -ordered[:, : 2 * LANES]], axis=1
+        )
+        by_column = jnp.swapaxes(ordered.reshape(rows, cols, own_count, 5 * LANES), 0, 1)
+        by_column = by_column.reshape(channels, 5 * LANES).astype(bf16)
+        for p, left in enumerate((ordered, rotated)):
+            cross = lax.dot_general(
+                left.astype(bf16), by_column, (((1,), (1,)), ((), ())), preferred_element_type=f32
+            ).astype(bf16)
+            width = channels // cols
+            for r in range(rows):
+                for c in range(cols):
+                    send2[r * cols + c, (2 * b + p) * block : (2 * b + p + 1) * block, :] = cross[
+                        r * block : (r + 1) * block, c * width : (c + 1) * width
+                    ]
+
+    def start_second(step, carry):
+        second(step).start()
+        return carry
+
+    lax.fori_loop(1, count, start_second, 0)
+    kept = pltpu.make_async_copy(send2.at[me], recv2.at[me], own.at[1])
+    kept.start()
+    kept.wait()
+
+    def wait_second(step, carry):
+        other, target = peer(step)
+        remote(send2.at[other], recv2.at[other], s2.at[other], r2.at[other], target).wait()
+        return carry
+
+    lax.fori_loop(1, count, wait_second, 0)
+
+    wide2[...] = recv2[...].astype(f32).reshape(wide2.shape)
+    column = lax.broadcasted_iota(jnp.int32, (1, LANES), 1)
+    for a in range(block):
+        piece = wide2[pl.ds(a, 2 * FREQS, stride=block), :].astype(bf16)
+        answer = jnp.dot(lags[...], piece, preferred_element_type=f32)[:LAGS]
+        same = (column // own_count == row_index) & (
+            col_index * own_count + column % own_count == a
+        )
+        lagged[pl.ds(a, LAGS, stride=block), :] = jnp.where(same, 0.0, answer)
+    out[...] = lagged[...].reshape(out.shape)
+
+
+def exchange_body(rows, cols, traces, slot_channel, usable_blocks):
+    own_count = traces.shape[0]
+    segment_total = traces.shape[1] // SEG
+    count = rows * cols
+    bins = FREQS // count
+    block = own_count * cols
+    channels = own_count * count
+    group = bins * own_count
+    table, taper = spectrum_table()
+    vmem = pl.BlockSpec(memory_space=pltpu.VMEM)
+    smem = pl.BlockSpec(memory_space=pltpu.SMEM)
+    f32, bf16 = jnp.float32, jnp.bfloat16
+    return pl.pallas_call(
+        functools.partial(exchange_kernel, rows, cols),
+        out_shape=jax.ShapeDtypeStruct((LAGS, block, channels // cols), f32),
+        in_specs=[vmem, smem, smem, vmem, vmem, vmem],
+        out_specs=vmem,
+        scratch_shapes=[
+            pltpu.VMEM((SPAN_SEGS * own_count, WIDE), bf16),
+            pltpu.VMEM((SPAN_SEGS * own_count, LANES), f32),
+            pltpu.VMEM((segment_total * own_count, LANES), f32),
+            pltpu.VMEM((5, FREQS * own_count, LANES), f32),
+            pltpu.VMEM((count, group, 5 * LANES), bf16),
+            pltpu.VMEM((count, group, 5 * LANES), bf16),
+            pltpu.VMEM((group, LANES), jnp.int32),
+            pltpu.VMEM((count, group, LANES), jnp.int32),
+            pltpu.VMEM((count, 2 * bins * block, LANES), bf16),
+            pltpu.VMEM((count, 2 * bins * block, LANES), bf16),
+            pltpu.VMEM((2 * FREQS * block, LANES), f32),
+            pltpu.VMEM((LAGS * block, LANES), f32),
+        ]
+        + [pltpu.SemaphoreType.DMA((count,))] * 6
+        + [pltpu.SemaphoreType.DMA((2,))],
+        compiler_params=pltpu.CompilerParams(
+            collective_id=0, has_side_effects=True, vmem_limit_bytes=40 * 1024 * 1024
+        ),
+    )(traces, slot_channel, usable_blocks, jnp.asarray(table), jnp.asarray(taper),
+      jnp.asarray(lag_table(segment_total)))
+
+
+def plan(rows, cols, freqs, traces, slot_channel, usable_blocks):
+    count = rows * cols
+    fits = (
+        freqs == 1
+        and FREQS % count == 0
+        and traces.shape[0] == 8
+        and rows * traces.shape[0] == LANES
+        and FREQS // count * traces.shape[0] % 16 == 0
+        and traces.shape[1] == (2 * LANES + HALF) * SEG
+    )
+    if fits:
+        return exchange_body(rows, cols, traces, slot_channel, usable_blocks)
+    return gather_body(traces, slot_channel, usable_blocks)
+
+
 def solution(mesh):
+    body = functools.partial(plan, *(mesh.shape[a] for a in ("row", "col", "freq")))
     in_specs = (
         P(("groups", "row", "col"), None),
         P(("groups", "row", "col")),

time: 154 us -> 57.2 us (0.37)
  the two profiles are of different devices: /device:TPU:0 before, /device:TPU:29 now
where the time goes in v1:
time: 57.2 us; the launch traced here: 56.9 us
  Pallas kernels  51.1 us (89%)
  local copies, waits for them, and re-layouts  5.17 us (9%)
  between operations  0.67 us (1%)
    pallas_call x1, Pallas kernels, exchange_body(): pl.pallas_call(functools.partial(exchange_kernel, rows, cols), out_shape=...  51.1 us
    unnamed x11, local copies, waits for them, and re-layouts  5.17 us

profile of v1, /device:TPU:29, one launch (start us, length us, event | category | flops | bytes accessed | tf_op | source)
XLA Modules:
  0.0 56.9 jit_solution(17333766853591109338)
XLA Ops:
  0.7 0.0 copy-start
  0.7 1.4 %copy-done = bf16[8,96000]{1,0:T(8,128)(2,1)S(1)} copy-done((bf16[8,96000]{1,0:T(8,128)(2,1)S(1)}, bf16[8,96000]{1,0:T(8,128)(2,1)}, u32[]{:S(2)}) %copy-start) | copy-done | bytes 1536024
  2.0 0.0 copy-start.1
  2.0 0.9 %copy-done.1 = bf16[384,128]{1,0:T(8,128)(2,1)S(1)} copy-done((bf16[384,128]{1,0:T(8,128)(2,1)S(1)}, bf16[384,128]{1,0:T(8,128)(2,1)}, u32[]{:S(2)}) %copy-start.1) | copy-done | bytes 98328
  2.9 0.0 copy-start.2
  2.9 0.7 %copy-done.2 = bf16[80,128]{1,0:T(8,128)(2,1)S(1)} copy-done((bf16[80,128]{1,0:T(8,128)(2,1)S(1)}, bf16[80,128]{1,0:T(8,128)(2,1)}, u32[]{:S(2)}) %copy-start.2) | copy-done | bytes 20504
  3.7 0.0 copy-start.3
  3.7 0.7 %copy-done.3 = f32[8,384]{1,0:T(8,128)S(1)} copy-done((f32[8,384]{1,0:T(8,128)S(1)}, f32[8,384]{1,0:T(8,128)}, u32[]{:S(2)}) %copy-start.3) | copy-done | bytes 12312
  4.4 0.0 copy-start.4
  4.4 0.7 %copy-done.4 = s32[8]{0:T(128)S(1)} copy-done((s32[8]{0:T(128)S(1)}, s32[8]{0:T(128)}, u32[]{:S(2)}) %copy-start.4) | copy-done | bytes 56
  5.0 51.1 %shard_map.64 = f32[65,16,128]{2,1,0:T(8,128)S(1)} custom-call(bf16[8,96000]{1,0:T(8,128)(2,1)S(1)} %copy-done, s32[8]{0:T(128)S(1)} %copy-done.4, s32[1]{0:T(128)S(6)} %copy.8.usable, bf16[384,128]{1,0:T(8,128)(2,1)S(1)} %copy-done.1, f32[8,384]{1,0:T(8,128)S(1)} %copy-done.3, bf16[80,128]{1,0:T(8,128)(2,1)S(1)} %copy-done.2), custom_call_target="tpu_custom_call" | custom-call | tf_op jit(solution)/shard_map/pallas_call | solution.py:316
  56.1 0.8 %copy.9 = f32[65,16,128]{2,1,0:T(8,128)} copy(f32[65,16,128]{2,1,0:T(8,128)S(1)} %shard_map.64) | data formatting | bytes 1064960
Async XLA Ops:
  0.7 1.4 %copy-start = (bf16[8,96000]{1,0:T(8,128)(2,1)S(1)}, bf16[8,96000]{1,0:T(8,128)(2,1)}, u32[]{:S(2)}) copy-start(bf16[8,96000]{1,0:T(8,128)(2,1)} %traces.1) | copy-start | bytes 4608004
  2.0 0.9 %copy-start.1 = (bf16[384,128]{1,0:T(8,128)(2,1)S(1)}, bf16[384,128]{1,0:T(8,128)(2,1)}, u32[]{:S(2)}) copy-start(bf16[384,128]{1,0:T(8,128)(2,1)} %constant.6.clone.table) | copy-start | bytes 294916
  2.9 0.7 %copy-start.2 = (bf16[80,128]{1,0:T(8,128)(2,1)S(1)}, bf16[80,128]{1,0:T(8,128)(2,1)}, u32[]{:S(2)}) copy-start(bf16[80,128]{1,0:T(8,128)(2,1)} %constant.8.clone.lags) | copy-start | bytes 61444
  3.7 0.7 %copy-start.3 = (f32[8,384]{1,0:T(8,128)S(1)}, f32[8,384]{1,0:T(8,128)}, u32[]{:S(2)}) copy-start(f32[8,384]{1,0:T(8,128)} %constant.7.clone.taper) | copy-start | bytes 36868
  4.4 0.7 %copy-start.4 = (s32[8]{0:T(128)S(1)}, s32[8]{0:T(128)}, u32[]{:S(2)}) copy-start(s32[8]{0:T(128)} %slots.1) | copy-start | bytes 100

commit v2 on v1

--- a/solution.py
+++ b/solution.py
@@ -119,20 +119,25 @@
     return table.astype(jnp.bfloat16), wide_taper
 
 
-def lag_table(segment_total):
+def lag_table(segment_total, bins):
     turns = (np.arange(LAGS) - MAXLAG)[:, None] * np.arange(1, FREQS + 1)[None, :] % SEG
     angles = 2.0 * np.pi / SEG * turns
     gain = corr_gain / math.sqrt(segment_total * FREQS)
     table = np.zeros((LAG_ROWS, FREQS, 2), np.float32)
     table[:LAGS, :, 0] = gain * np.cos(angles)
     table[:LAGS, :, 1] = -gain * np.sin(angles)
+    table = table.reshape(LAG_ROWS, FREQS // bins, bins, 2).transpose(0, 2, 1, 3)
     return table.reshape(LAG_ROWS, 2 * FREQS).astype(jnp.bfloat16)
 
 
+PARTS = ((0, 4, (0, 3)), (4, 8, (1, 4)), (8, 10, (2,)))
+
+
 def exchange_kernel(
-    rows, cols, traces, slots, usable, table, taper, lags, out,
-    samples, levels, white, spectra, send1, recv1, meta, recv_meta, send2, recv2, wide2, lagged,
-    s1, r1, sm, rm, s2, r2, own,
+    rows, cols, traces_in, slots, usable, table_in, taper_in, lags_in, out,
+    traces, table, taper, lags, samples, powers, white, spectra,
+    send_a, send_b, send_c, recv_a, recv_b, recv_c, meta, recv_meta, picks, totals,
+    send2, recv2, wide2, lagged, s1, r1, sm, rm, s2, r2, own,
 ):
     f32, bf16 = jnp.float32, jnp.bfloat16
     count = rows * cols
@@ -141,9 +146,21 @@
     block = own_count * cols
     channels = own_count * count
     group = bins * own_count
-    spans = traces.shape[1] // SPAN
+    width = channels // cols
     row_index, col_index = lax.axis_index("row"), lax.axis_index("col")
     me = row_index * cols + col_index
+    sends, recvs = (send_a, send_b, send_c), (recv_a, recv_b, recv_c)
+
+    fetches = []
+    for number, (low, high, _) in enumerate(PARTS):
+        span = pl.ds(low * SPAN, (high - low) * SPAN)
+        fetches.append(
+            pltpu.make_async_copy(traces_in.at[:, span], traces.at[:, span], own.at[number])
+        )
+    for number, (source, place) in enumerate(((table_in, table), (taper_in, taper), (lags_in, lags))):
+        fetches.append(pltpu.make_async_copy(source, place, own.at[3 + number]))
+    for number in (4, 0, 3, 1, 2, 5):
+        fetches[number].start()
 
     def peer(step):
         other = lax.rem(me + step, count)
@@ -159,13 +176,17 @@
 
     lax.fori_loop(1, count, greet, 0)
 
-    sub = lax.broadcasted_iota(jnp.int32, (group, LANES), 0)
-    lane = lax.broadcasted_iota(jnp.int32, (group, LANES), 1)
-    place = jnp.zeros((group, LANES), jnp.int32)
+    def remote(src, dst, send_sem, recv_sem, target):
+        return pltpu.make_async_remote_copy(
+            src_ref=src, dst_ref=dst, send_sem=send_sem, recv_sem=recv_sem,
+            device_id=target, device_id_type=pl.DeviceIdType.MESH,
+        )
+
+    lane = lax.broadcasted_iota(jnp.int32, (1, LANES), 1)
+    row = jnp.where(lane == own_count, usable[0], 0)
     for u in range(own_count):
-        place = jnp.where(sub % own_count == u, slots[u], place)
-    place = place + sub // own_count * channels
-    meta[...] = jnp.where(lane < HALF, place, usable[0])
+        row = jnp.where(lane == u, slots[u], row)
+    meta[...] = row
 
     def one_span(span, carry):
         for s in range(0, SPAN_SEGS, 2):
@@ -173,123 +194,163 @@
             for q in (s, s + 1):
                 base = q * SEG // LANES * LANES
                 shift = q * SEG - base
-                width = -(-(shift + SEG) // LANES) * LANES
-                x = traces[:, pl.ds(pl.multiple_of(span * SPAN + base, LANES), width)].astype(f32)
+                reach = -(-(shift + SEG) // LANES) * LANES
+                x = traces[:, pl.ds(pl.multiple_of(span * SPAN + base, LANES), reach)].astype(f32)
                 if shift:
-                    x = pltpu.roll(x, width - shift, 1)
+                    x = pltpu.roll(x, reach - shift, 1)
                 x = x[:, :WIDE]
                 windowed = x * taper[...]
-                power = jnp.sum(windowed * windowed, axis=1, keepdims=True)
-                level = water_level * jnp.sqrt(power + SEG * 1e-05)
-                levels[q * own_count : (q + 1) * own_count, :] = jnp.broadcast_to(
-                    level, (own_count, LANES)
-                )
+                square = windowed * windowed
+                power = square[:, :LANES]
+                for t in range(1, WIDE // LANES):
+                    power = power + square[:, t * LANES : (t + 1) * LANES]
+                powers[q * own_count : (q + 1) * own_count, :] = power
                 pair.append(x)
             samples[s * own_count : (s + 2) * own_count, :] = jnp.concatenate(pair, 0).astype(bf16)
         y = jnp.dot(samples[...], table[...], preferred_element_type=f32)
+        ones = jnp.ones((LANES, LANES), bf16)
+        power = powers[...]
+        high = power.astype(bf16)
+        rest = (power - high.astype(f32)).astype(bf16)
+        power = jnp.dot(high, ones, preferred_element_type=f32) + jnp.dot(
+            rest, ones, preferred_element_type=f32
+        )
+        level = water_level * jnp.sqrt(power + SEG * 1e-05)
         square = y * y
         magnitude = jnp.sqrt(square + pltpu.roll(square, FREQS, 1))
         depth = SPAN_SEGS * own_count
-        white[pl.ds(pl.multiple_of(span * depth, depth), depth), :] = y / (magnitude + levels[...])
+        white[pl.ds(pl.multiple_of(span * depth, depth), depth), :] = y / (magnitude + level)
         return carry
 
-    lax.fori_loop(0, spans, one_span, 0)
-
-    for u in range(own_count):
-        strip = pl.ds(u, FREQS, stride=own_count)
-        for t in range(2):
-            z = white[pl.ds(t * LANES * own_count + u, LANES, stride=own_count), :].T
-            spectra[t, strip, :] = z[:FREQS]
-            spectra[3 + t, strip, :] = z[FREQS:]
-        z = white[pl.ds(2 * LANES * own_count + u, HALF, stride=own_count), :]
-        z = jnp.concatenate([z, pltpu.roll(z, FREQS, 1)], 0).T
-        spectra[2, strip, :] = z[:FREQS]
-    for t in range(5):
-        send1[:, :, t * LANES : (t + 1) * LANES] = (
-            spectra[t].astype(bf16).reshape(count, group, LANES)
-        )
-
-    pl.semaphore_wait(barrier, count - 1)
-
-    def remote(src, dst, send_sem, recv_sem, target):
-        return pltpu.make_async_remote_copy(
-            src_ref=src, dst_ref=dst, send_sem=send_sem, recv_sem=recv_sem,
-            device_id=target, device_id_type=pl.DeviceIdType.MESH,
-        )
-
-    def first(step):
-        other, target = peer(step)
-        return (
-            remote(meta, recv_meta.at[me], sm.at[other], rm.at[me], target),
-            remote(send1.at[other], recv1.at[me], s1.at[other], r1.at[me], target),
-        )
-
-    def second(step):
-        other, target = peer(step)
-        return remote(send2.at[other], recv2.at[me], s2.at[other], r2.at[me], target)
-
-    def start_first(step, carry):
-        for copy in first(step):
-            copy.start()
-        return carry
-
-    lax.fori_loop(1, count, start_first, 0)
-    kept = pltpu.make_async_copy(send1.at[me], recv1.at[me], own.at[0])
-    kept.start()
-    recv_meta[me] = meta[...]
-    kept.wait()
-
-    def wait_first(step, carry):
+    fetches[4].wait()
+    fetches[3].wait()
+    for number, (low, high, tiles) in enumerate(PARTS):
+        fetches[number].wait()
+        lax.fori_loop(low, high, one_span, 0)
+        send, recv = sends[number], recvs[number]
+        for u in range(own_count):
+            strip = pl.ds(u, FREQS, stride=own_count)
+            depth = (high - low) * SPAN_SEGS
+            z = white[pl.ds(low * SPAN_SEGS * own_count + u, depth, stride=own_count), :]
+            if len(tiles) == 1:
+                z = jnp.concatenate([z, pltpu.roll(z, FREQS, 1)], 0)
+            z = z.T
+            for half in range(len(tiles)):
+                spectra[half, strip, :] = z[half * FREQS : (half + 1) * FREQS]
+        for half in range(len(tiles)):
+            send[:, :, half * LANES : (half + 1) * LANES] = (
+                spectra[half].astype(bf16).reshape(count, group, LANES)
+            )
+        if number == 0:
+            pl.semaphore_wait(barrier, count - 1)
+
+            def start_meta(step, carry):
+                other, target = peer(step)
+                remote(meta, recv_meta.at[me], sm.at[other], rm.at[me], target).start()
+                return carry
+
+            lax.fori_loop(1, count, start_meta, 0)
+            recv_meta[me] = meta[...]
+
+        def start_part(step, carry):
+            other, target = peer(step)
+            remote(
+                send.at[other], recv.at[me], s1.at[number, other], r1.at[number, me], target
+            ).start()
+            return carry
+
+        lax.fori_loop(1, count, start_part, 0)
+        recv[me] = send[me]
+
+    def wait_meta(step, carry):
         other, target = peer(step)
         remote(meta, recv_meta.at[other], sm.at[other], rm.at[other], target).wait()
-        remote(send1.at[other], recv1.at[other], s1.at[other], r1.at[other], target).wait()
         return carry
 
-    lax.fori_loop(1, count, wait_first, 0)
-
-    known = recv_meta[...]
-    target_row = known.reshape(count * group, LANES).astype(f32).T[0:1, :]
-    good = known[:, :own_count, HALF : HALF + 1].reshape(channels, 1).astype(f32)
-    gathered = recv1[...].reshape(count * group, 5 * LANES)
-    lane_sign = jnp.where(lax.broadcasted_iota(jnp.int32, (1, LANES), 1) < HALF, 1.0, -1.0)
+    lax.fori_loop(1, count, wait_meta, 0)
+    total = count * group
+    known = recv_meta[...].reshape(count, LANES).astype(f32).astype(bf16)
+    expand = (
+        lax.broadcasted_iota(jnp.int32, (LANES, total), 0)
+        == lax.broadcasted_iota(jnp.int32, (LANES, total), 1) % own_count
+    )
+    spread = jnp.dot(known, jnp.where(expand, 1.0, 0.0).astype(bf16), preferred_element_type=f32)
+    source = lax.broadcasted_iota(jnp.int32, (count, total), 1) // group
+    mine = source == lax.broadcasted_iota(jnp.int32, (count, total), 0)
+    target_row = jnp.sum(jnp.where(mine, spread, 0.0), axis=0, keepdims=True)
+    holder = lax.broadcasted_iota(jnp.int32, (channels, count), 0) // own_count
+    holder = holder == lax.broadcasted_iota(jnp.int32, (channels, count), 1)
+    good = jnp.dot(jnp.where(holder, 1.0, 0.0).astype(bf16), known, preferred_element_type=f32)
+    good = good[:, own_count : own_count + 1]
+    row_number = lax.broadcasted_iota(jnp.int32, (channels, 1), 0).astype(f32)
+    bin_number = lax.broadcasted_iota(jnp.int32, (1, total), 1) // own_count % bins
     for b in range(bins):
-        row_number = lax.broadcasted_iota(jnp.int32, (channels, 1), 0) + b * channels
-        pick = jnp.where(row_number.astype(f32) == target_row, good, 0.0).astype(bf16)
-        ordered = jnp.dot(pick, gathered, preferred_element_type=f32)
-        mid = pltpu.roll(ordered[:, 2 * LANES : 3 * LANES], HALF, 1) * lane_sign
-        rotated = jnp.concatenate(
-            [ordered[:, 3 * LANES :], mid, -ordered[:, : 2 * LANES]], axis=1
-        )
-        by_column = jnp.swapaxes(ordered.reshape(rows, cols, own_count, 5 * LANES), 0, 1)
-        by_column = by_column.reshape(channels, 5 * LANES).astype(bf16)
-        for p, left in enumerate((ordered, rotated)):
-            cross = lax.dot_general(
-                left.astype(bf16), by_column, (((1,), (1,)), ((), ())), preferred_element_type=f32
-            ).astype(bf16)
-            width = channels // cols
-            for r in range(rows):
-                for c in range(cols):
-                    send2[r * cols + c, (2 * b + p) * block : (2 * b + p + 1) * block, :] = cross[
-                        r * block : (r + 1) * block, c * width : (c + 1) * width
-                    ]
-
-    def start_second(step, carry):
-        second(step).start()
-        return carry
-
-    lax.fori_loop(1, count, start_second, 0)
-    kept = pltpu.make_async_copy(send2.at[me], recv2.at[me], own.at[1])
-    kept.start()
-    kept.wait()
-
-    def wait_second(step, carry):
-        other, target = peer(step)
-        remote(send2.at[other], recv2.at[other], s2.at[other], r2.at[other], target).wait()
-        return carry
-
-    lax.fori_loop(1, count, wait_second, 0)
-
-    wide2[...] = recv2[...].astype(f32).reshape(wide2.shape)
+        found = (row_number == target_row) & (bin_number == b)
+        picks[b] = jnp.where(found, good, 0.0).astype(bf16)
+
+    def start_second(b):
+        def body(step, carry):
+            other, target = peer(step)
+            remote(
+                send2.at[b, other], recv2.at[b, me], s2.at[b, other], r2.at[b, me], target
+            ).start()
+            return carry
+
+        lax.fori_loop(1, count, body, 0)
+        recv2[b, me] = send2[b, me]
+
+    for number, (low, high, tiles) in enumerate(PARTS):
+        send, recv = sends[number], recvs[number]
+
+        def wait_part(step, carry):
+            other, target = peer(step)
+            remote(
+                send.at[other], recv.at[other], s1.at[number, other], r1.at[number, other], target
+            ).wait()
+            return carry
+
+        lax.fori_loop(1, count, wait_part, 0)
+        depth = len(tiles) * LANES
+        gathered = recv[...].reshape(total, depth)
+        for b in range(bins):
+            ordered = jnp.dot(picks[b], gathered, preferred_element_type=f32)
+            turned = pltpu.roll(ordered, depth // 2, 1)
+            sign = lax.broadcasted_iota(jnp.int32, (1, depth), 1) < depth // 2
+            rotated = turned * jnp.where(sign, 1.0, -1.0)
+            by_column = jnp.swapaxes(ordered.reshape(rows, cols, own_count, depth), 0, 1)
+            by_column = by_column.reshape(channels, depth).astype(bf16)
+            for p, left in enumerate((ordered, rotated)):
+                cross = lax.dot_general(
+                    left.astype(bf16), by_column, (((1,), (1,)), ((), ())),
+                    preferred_element_type=f32,
+                )
+                if number > 0:
+                    cross = cross + totals[2 * b + p]
+                if number < len(PARTS) - 1:
+                    totals[2 * b + p] = cross
+                    continue
+                cross = cross.astype(bf16)
+                for r in range(rows):
+                    for c in range(cols):
+                        send2[b, r * cols + c, p * block : (p + 1) * block, :] = cross[
+                            r * block : (r + 1) * block, c * width : (c + 1) * width
+                        ]
+            if number == len(PARTS) - 1:
+                start_second(b)
+
+    for b in range(bins):
+
+        def wait_second(step, carry):
+            other, target = peer(step)
+            remote(
+                send2.at[b, other], recv2.at[b, other], s2.at[b, other], r2.at[b, other], target
+            ).wait()
+            return carry
+
+        lax.fori_loop(1, count, wait_second, 0)
+        depth = count * 2 * block
+        wide2[b * depth : (b + 1) * depth, :] = recv2[b].astype(f32).reshape(depth, LANES)
+    fetches[5].wait()
     column = lax.broadcasted_iota(jnp.int32, (1, LANES), 1)
     for a in range(block):
         piece = wide2[pl.ds(a, 2 * FREQS, stride=block), :].astype(bf16)
@@ -310,35 +371,50 @@
     channels = own_count * count
     group = bins * own_count
     table, taper = spectrum_table()
+    lags = lag_table(segment_total, bins)
     vmem = pl.BlockSpec(memory_space=pltpu.VMEM)
     smem = pl.BlockSpec(memory_space=pltpu.SMEM)
+    anywhere = pl.BlockSpec(memory_space=pl.ANY)
     f32, bf16 = jnp.float32, jnp.bfloat16
+    part_shapes = [(count, group, len(tiles) * LANES) for _, _, tiles in PARTS]
     return pl.pallas_call(
         functools.partial(exchange_kernel, rows, cols),
         out_shape=jax.ShapeDtypeStruct((LAGS, block, channels // cols), f32),
-        in_specs=[vmem, smem, smem, vmem, vmem, vmem],
+        in_specs=[anywhere, smem, smem, anywhere, anywhere, anywhere],
         out_specs=vmem,
         scratch_shapes=[
+            pltpu.VMEM(traces.shape, bf16),
+            pltpu.VMEM(table.shape, bf16),
+            pltpu.VMEM(taper.shape, f32),
+            pltpu.VMEM(lags.shape, bf16),
             pltpu.VMEM((SPAN_SEGS * own_count, WIDE), bf16),
             pltpu.VMEM((SPAN_SEGS * own_count, LANES), f32),
             pltpu.VMEM((segment_total * own_count, LANES), f32),
-            pltpu.VMEM((5, FREQS * own_count, LANES), f32),
-            pltpu.VMEM((count, group, 5 * LANES), bf16),
-            pltpu.VMEM((count, group, 5 * LANES), bf16),
-            pltpu.VMEM((group, LANES), jnp.int32),
-            pltpu.VMEM((count, group, LANES), jnp.int32),
-            pltpu.VMEM((count, 2 * bins * block, LANES), bf16),
-            pltpu.VMEM((count, 2 * bins * block, LANES), bf16),
+            pltpu.VMEM((2, FREQS * own_count, LANES), f32),
+        ]
+        + [pltpu.VMEM(shape, bf16) for shape in part_shapes + part_shapes]
+        + [
+            pltpu.VMEM((1, LANES), jnp.int32),
+            pltpu.VMEM((count, 1, LANES), jnp.int32),
+            pltpu.VMEM((bins, channels, count * group), bf16),
+            pltpu.VMEM((2 * bins, channels, channels), f32),
+            pltpu.VMEM((bins, count, 2 * block, LANES), bf16),
+            pltpu.VMEM((bins, count, 2 * block, LANES), bf16),
             pltpu.VMEM((2 * FREQS * block, LANES), f32),
             pltpu.VMEM((LAGS * block, LANES), f32),
-        ]
-        + [pltpu.SemaphoreType.DMA((count,))] * 6
-        + [pltpu.SemaphoreType.DMA((2,))],
+            pltpu.SemaphoreType.DMA((len(PARTS), count)),
+            pltpu.SemaphoreType.DMA((len(PARTS), count)),
+            pltpu.SemaphoreType.DMA((count,)),
+            pltpu.SemaphoreType.DMA((count,)),
+            pltpu.SemaphoreType.DMA((bins, count)),
+            pltpu.SemaphoreType.DMA((bins, count)),
+            pltpu.SemaphoreType.DMA((6,)),
+        ],
         compiler_params=pltpu.CompilerParams(
             collective_id=0, has_side_effects=True, vmem_limit_bytes=40 * 1024 * 1024
         ),
     )(traces, slot_channel, usable_blocks, jnp.asarray(table), jnp.asarray(taper),
-      jnp.asarray(lag_table(segment_total)))
+      jnp.asarray(lags))
 
 
 def plan(rows, cols, freqs, traces, slot_channel, usable_blocks):

time: 57.2 us -> 48.5 us (0.85)
  the two profiles are of different devices: /device:TPU:29 before, /device:TPU:0 now
where the time goes in v2:
time: 48.5 us; the launch traced here: 48.2 us
  Pallas kernels  42.3 us (87%)
  local copies, waits for them, and re-layouts  5.17 us (11%)
  between operations  0.67 us (1%)
    pallas_call x1, Pallas kernels, exchange_body(): pl.pallas_call(functools.partial(exchange_kernel, rows, cols), out_shape=...  42.3 us
    unnamed x11, local copies, waits for them, and re-layouts  5.17 us

profile of v2, /device:TPU:0, one launch (start us, length us, event | category | flops | bytes accessed | tf_op | source)
XLA Modules:
  0.0 48.2 jit_solution(9624525970159723802)
XLA Ops:
  0.7 0.0 copy-start
  0.7 1.4 %copy-done = bf16[8,96000]{1,0:T(8,128)(2,1)S(1)} copy-done((bf16[8,96000]{1,0:T(8,128)(2,1)S(1)}, bf16[8,96000]{1,0:T(8,128)(2,1)}, u32[]{:S(2)}) %copy-start) | copy-done | bytes 1536024
  2.0 0.0 copy-start.1
  2.0 0.9 %copy-done.1 = bf16[384,128]{1,0:T(8,128)(2,1)S(1)} copy-done((bf16[384,128]{1,0:T(8,128)(2,1)S(1)}, bf16[384,128]{1,0:T(8,128)(2,1)}, u32[]{:S(2)}) %copy-start.1) | copy-done | bytes 98328
  2.9 0.0 copy-start.2
  2.9 0.7 %copy-done.2 = bf16[80,128]{1,0:T(8,128)(2,1)S(1)} copy-done((bf16[80,128]{1,0:T(8,128)(2,1)S(1)}, bf16[80,128]{1,0:T(8,128)(2,1)}, u32[]{:S(2)}) %copy-start.2) | copy-done | bytes 20504
  3.7 0.0 copy-start.3
  3.7 0.7 %copy-done.3 = f32[8,384]{1,0:T(8,128)S(1)} copy-done((f32[8,384]{1,0:T(8,128)S(1)}, f32[8,384]{1,0:T(8,128)}, u32[]{:S(2)}) %copy-start.3) | copy-done | bytes 12312
  4.4 0.0 copy-start.4
  4.4 0.7 %copy-done.4 = s32[8]{0:T(128)S(1)} copy-done((s32[8]{0:T(128)S(1)}, s32[8]{0:T(128)}, u32[]{:S(2)}) %copy-start.4) | copy-done | bytes 56
  5.0 42.3 %shard_map.64 = f32[65,16,128]{2,1,0:T(8,128)S(1)} custom-call(bf16[8,96000]{1,0:T(8,128)(2,1)S(1)} %copy-done, s32[8]{0:T(128)S(1)} %copy-done.4, s32[1]{0:T(128)S(6)} %copy.8.usable, bf16[384,128]{1,0:T(8,128)(2,1)S(1)} %copy-done.1, f32[8,384]{1,0:T(8,128)S(1)} %copy-done.3, bf16[80,128]{1,0:T(8,128)(2,1)S(1)} %copy-done.2), custom_call_target="tpu_custom_call" | custom-call | tf_op jit(solution)/shard_map/pallas_call | solution.py:380
  47.4 0.8 %copy.9 = f32[65,16,128]{2,1,0:T(8,128)} copy(f32[65,16,128]{2,1,0:T(8,128)S(1)} %shard_map.64) | data formatting | bytes 1064960
Async XLA Ops:
  0.7 1.4 %copy-start = (bf16[8,96000]{1,0:T(8,128)(2,1)S(1)}, bf16[8,96000]{1,0:T(8,128)(2,1)}, u32[]{:S(2)}) copy-start(bf16[8,96000]{1,0:T(8,128)(2,1)} %traces_in.1) | copy-start | bytes 4608004
  2.0 0.9 %copy-start.1 = (bf16[384,128]{1,0:T(8,128)(2,1)S(1)}, bf16[384,128]{1,0:T(8,128)(2,1)}, u32[]{:S(2)}) copy-start(bf16[384,128]{1,0:T(8,128)(2,1)} %constant.6.clone.table_in) | copy-start | bytes 294916
  2.9 0.7 %copy-start.2 = (bf16[80,128]{1,0:T(8,128)(2,1)S(1)}, bf16[80,128]{1,0:T(8,128)(2,1)}, u32[]{:S(2)}) copy-start(bf16[80,128]{1,0:T(8,128)(2,1)} %constant.8.clone.lags_in) | copy-start | bytes 61444
  3.7 0.7 %copy-start.3 = (f32[8,384]{1,0:T(8,128)S(1)}, f32[8,384]{1,0:T(8,128)}, u32[]{:S(2)}) copy-start(f32[8,384]{1,0:T(8,128)} %constant.7.clone.taper_in) | copy-start | bytes 36868
  4.4 0.7 %copy-start.4 = (s32[8]{0:T(128)S(1)}, s32[8]{0:T(128)}, u32[]{:S(2)}) copy-start(s32[8]{0:T(128)} %slots.1) | copy-start | bytes 100

commit v3 on v2

--- a/solution.py
+++ b/solution.py
@@ -374,7 +374,7 @@
     lags = lag_table(segment_total, bins)
     vmem = pl.BlockSpec(memory_space=pltpu.VMEM)
     smem = pl.BlockSpec(memory_space=pltpu.SMEM)
-    anywhere = pl.BlockSpec(memory_space=pl.ANY)
+    anywhere = pl.BlockSpec(memory_space=pltpu.HBM)
     f32, bf16 = jnp.float32, jnp.bfloat16
     part_shapes = [(count, group, len(tiles) * LANES) for _, _, tiles in PARTS]
     return pl.pallas_call(
@@ -411,7 +411,7 @@
             pltpu.SemaphoreType.DMA((6,)),
         ],
         compiler_params=pltpu.CompilerParams(
-            collective_id=0, has_side_effects=True, vmem_limit_bytes=40 * 1024 * 1024
+            collective_id=0, has_side_effects=True, vmem_limit_bytes=60 * 1024 * 1024
         ),
     )(traces, slot_channel, usable_blocks, jnp.asarray(table), jnp.asarray(taper),
       jnp.asarray(lags))

time: 48.5 us -> 45.5 us (0.938)
  local copies, waits for them, and re-layouts: 5.17 us -> 1.87 us
    unnamed x11 -> x1, local copies, waits for them, and re-layouts: 5.17 us -> 1.87 us
where the time goes in v3:
time: 45.5 us; the launch traced here: 45.3 us
  Pallas kernels  42.7 us (94%)
  local copies, waits for them, and re-layouts  1.87 us (4%)
  between operations  0.66 us (1%)
    pallas_call x1, Pallas kernels, exchange_body(): pl.pallas_call(functools.partial(exchange_kernel, rows, cols), out_shape=...  42.7 us
    unnamed x1, local copies, waits for them, and re-layouts  1.87 us

profile of v3, /device:TPU:0, one launch (start us, length us, event | category | flops | bytes accessed | tf_op | source)
XLA Modules:
  0.0 45.3 jit_solution(1843480520390335554)
XLA Ops:
  0.7 42.7 %shard_map.64 = f32[65,16,128]{2,1,0:T(8,128)} custom-call(bf16[8,96000]{1,0:T(8,128)(2,1)} %traces_in.1, s32[8]{0:T(128)} %slots.1, s32[1]{0:T(128)S(6)} %copy.8.usable, bf16[384,128]{1,0:T(8,128)(2,1)} %constant.6.clone.table_in, f32[8,384]{1,0:T(8,128)} %constant.7.clone.taper_in, bf16[80,128]{1,0:T(8,128)(2,1)} %constant.8.clone.lags_in), custom_call_target="tpu_custom_call" | custom-call | tf_op jit(solution)/shard_map/pallas_call | solution.py:380
  43.4 1.9 %copy.9 = f32[65,16,128]{2,1,0:T(8,128)} copy(f32[65,16,128]{2,1,0:T(8,128)} %shard_map.64) | data formatting | bytes 1064960

commit v4 on v3

--- a/solution.py
+++ b/solution.py
@@ -126,8 +126,10 @@
     table = np.zeros((LAG_ROWS, FREQS, 2), np.float32)
     table[:LAGS, :, 0] = gain * np.cos(angles)
     table[:LAGS, :, 1] = -gain * np.sin(angles)
-    table = table.reshape(LAG_ROWS, FREQS // bins, bins, 2).transpose(0, 2, 1, 3)
-    return table.reshape(LAG_ROWS, 2 * FREQS).astype(jnp.bfloat16)
+    table = table.reshape(LAG_ROWS, -1, 2, bins, 2)
+    own = table.transpose(3, 0, 1, 2, 4).reshape(bins * LAG_ROWS, -1)
+    far = table.transpose(3, 0, 2, 1, 4).reshape(bins * LAG_ROWS, -1)
+    return np.stack([own, far]).astype(jnp.bfloat16)
 
 
 PARTS = ((0, 4, (0, 3)), (4, 8, (1, 4)), (8, 10, (2,)))
@@ -136,8 +138,10 @@
 def exchange_kernel(
     rows, cols, traces_in, slots, usable, table_in, taper_in, lags_in, out,
     traces, table, taper, lags, samples, powers, white, spectra,
-    send_a, send_b, send_c, recv_a, recv_b, recv_c, meta, recv_meta, picks, totals,
-    send2, recv2, wide2, lagged, s1, r1, sm, rm, s2, r2, own,
+    send_a, send_b, send_c, near_a, near_b, near_c, far_a, far_b, far_c, meta, recv_meta,
+    near_picks, far_picks, near_left, near_right, near_sum, out_sum, in_sum,
+    near_send, far_send, near_recv, far_recv, near_wide, far_wide, lagged,
+    s1n, r1n, s1f, r1f, sm, rm, s2n, r2n, s2f, r2f, own,
 ):
     f32, bf16 = jnp.float32, jnp.bfloat16
     count = rows * cols
@@ -146,10 +150,13 @@
     block = own_count * cols
     channels = own_count * count
     group = bins * own_count
-    width = channels // cols
+    members = count // 2
+    span_channels = channels // 2
     row_index, col_index = lax.axis_index("row"), lax.axis_index("col")
     me = row_index * cols + col_index
-    sends, recvs = (send_a, send_b, send_c), (recv_a, recv_b, recv_c)
+    side, member = me // members, lax.rem(me, members)
+    sends = (send_a, send_b, send_c)
+    nears, fars = (near_a, near_b, near_c), (far_a, far_b, far_c)
 
     fetches = []
     for number, (low, high, _) in enumerate(PARTS):
@@ -165,6 +172,11 @@
     def peer(step):
         other = lax.rem(me + step, count)
         return other, {"row": other // cols, "col": lax.rem(other, cols)}
+
+    def in_half(half, step):
+        place = lax.rem(member + step, members)
+        other = half * members + place
+        return place, {"row": other // cols, "col": lax.rem(other, cols)}
 
     barrier = pltpu.get_barrier_semaphore()
 
@@ -227,7 +239,7 @@
     for number, (low, high, tiles) in enumerate(PARTS):
         fetches[number].wait()
         lax.fori_loop(low, high, one_span, 0)
-        send, recv = sends[number], recvs[number]
+        send, near, far = sends[number], nears[number], fars[number]
         for u in range(own_count):
             strip = pl.ds(u, FREQS, stride=own_count)
             depth = (high - low) * SPAN_SEGS
@@ -252,15 +264,25 @@
             lax.fori_loop(1, count, start_meta, 0)
             recv_meta[me] = meta[...]
 
+        def start_far(step):
+            place, target = in_half(1 - side, step)
+            remote(
+                send.at[2 * place + 1 - side], far.at[member],
+                s1f.at[number, place], r1f.at[number, member], target,
+            ).start()
+
         def start_part(step, carry):
-            other, target = peer(step)
+            start_far(step)
+            place, target = in_half(side, step)
             remote(
-                send.at[other], recv.at[me], s1.at[number, other], r1.at[number, me], target
+                send.at[pl.ds(2 * place, 2)], near.at[member],
+                s1n.at[number, place], r1n.at[number, member], target,
             ).start()
             return carry
 
-        lax.fori_loop(1, count, start_part, 0)
-        recv[me] = send[me]
+        start_far(0)
+        lax.fori_loop(1, members, start_part, 0)
+        near[member] = send[pl.ds(2 * member, 2)]
 
     def wait_meta(step, carry):
         other, target = peer(step)
@@ -268,93 +290,173 @@
         return carry
 
     lax.fori_loop(1, count, wait_meta, 0)
-    total = count * group
     known = recv_meta[...].reshape(count, LANES).astype(f32).astype(bf16)
-    expand = (
-        lax.broadcasted_iota(jnp.int32, (LANES, total), 0)
-        == lax.broadcasted_iota(jnp.int32, (LANES, total), 1) % own_count
-    )
-    spread = jnp.dot(known, jnp.where(expand, 1.0, 0.0).astype(bf16), preferred_element_type=f32)
-    source = lax.broadcasted_iota(jnp.int32, (count, total), 1) // group
-    mine = source == lax.broadcasted_iota(jnp.int32, (count, total), 0)
-    target_row = jnp.sum(jnp.where(mine, spread, 0.0), axis=0, keepdims=True)
-    holder = lax.broadcasted_iota(jnp.int32, (channels, count), 0) // own_count
-    holder = holder == lax.broadcasted_iota(jnp.int32, (channels, count), 1)
-    good = jnp.dot(jnp.where(holder, 1.0, 0.0).astype(bf16), known, preferred_element_type=f32)
-    good = good[:, own_count : own_count + 1]
-    row_number = lax.broadcasted_iota(jnp.int32, (channels, 1), 0).astype(f32)
-    bin_number = lax.broadcasted_iota(jnp.int32, (1, total), 1) // own_count % bins
-    for b in range(bins):
-        found = (row_number == target_row) & (bin_number == b)
-        picks[b] = jnp.where(found, good, 0.0).astype(bf16)
-
-    def start_second(b):
-        def body(step, carry):
-            other, target = peer(step)
+
+    def choose(half, pieces, picks):
+        each = pieces * group
+        total = members * each
+        expand = (
+            lax.broadcasted_iota(jnp.int32, (LANES, total), 0)
+            == lax.broadcasted_iota(jnp.int32, (LANES, total), 1) % own_count
+        )
+        expand = jnp.where(expand, 1.0, 0.0).astype(bf16)
+        spread = jnp.dot(known, expand, preferred_element_type=f32)
+        source = lax.broadcasted_iota(jnp.int32, (count, total), 1) // each + half * members
+        mine = source == lax.broadcasted_iota(jnp.int32, (count, total), 0)
+        target_row = jnp.sum(jnp.where(mine, spread, 0.0), axis=0, keepdims=True)
+        holder = lax.broadcasted_iota(jnp.int32, (span_channels, count), 0) // own_count
+        holder = holder + half * members
+        holder = holder == lax.broadcasted_iota(jnp.int32, (span_channels, count), 1)
+        good = jnp.dot(jnp.where(holder, 1.0, 0.0).astype(bf16), known, preferred_element_type=f32)
+        good = good[:, own_count : own_count + 1]
+        row_number = lax.broadcasted_iota(jnp.int32, (span_channels, 1), 0) + half * span_channels
+        row_number = row_number.astype(f32)
+        bin_number = lax.broadcasted_iota(jnp.int32, (1, total), 1) // own_count % (pieces * bins)
+        for b in range(pieces * bins):
+            found = (row_number == target_row) & (bin_number == b)
+            picks[b] = jnp.where(found, good, 0.0).astype(bf16)
+
+    choose(side, 2, near_picks)
+    choose(1 - side, 1, far_picks)
+
+    def sides(pick, gathered):
+        depth = gathered.shape[1]
+        ordered = jnp.dot(pick, gathered, preferred_element_type=f32)
+        turned = pltpu.roll(ordered, depth // 2, 1)
+        sign = lax.broadcasted_iota(jnp.int32, (1, depth), 1) < depth // 2
+        rotated = turned * jnp.where(sign, 1.0, -1.0)
+        by_column = jnp.swapaxes(ordered.reshape(rows // 2, cols, own_count, depth), 0, 1)
+        left = jnp.concatenate([ordered.astype(bf16), rotated.astype(bf16)], 0)
+        return left, by_column.reshape(span_channels, depth).astype(bf16)
+
+    def pairs(left, right):
+        return lax.dot_general(
+            left, right, (((1,), (1,)), ((), ())), preferred_element_type=f32
+        )
+
+    first_lanes = lane < HALF
+
+    def place_units(even, odd, store):
+        units = (
+            jnp.where(first_lanes, even, pltpu.roll(odd, HALF, 1)).astype(bf16),
+            jnp.where(first_lanes, pltpu.roll(even, HALF, 1), odd).astype(bf16),
+        )
+        for c in range(cols):
+            for r in range(rows // 2):
+                for p in range(2):
+                    low = p * span_channels + r * block
+                    store(r * cols + c, p * block, units[c][low : low + block, :])
+
+    def store_far(place, low, unit):
+        far_send[place, low : low + block, :] = unit
+
+    def store_near(number):
+        def store(place, low, unit):
+            near_send[place, number, low : low + block, :] = unit
+
+        return store
+
+    for number, (_, _, tiles) in enumerate(PARTS):
+        send, near, far = sends[number], nears[number], fars[number]
+
+        def wait_far(step):
+            place, target = in_half(1 - side, step)
             remote(
-                send2.at[b, other], recv2.at[b, me], s2.at[b, other], r2.at[b, me], target
-            ).start()
-            return carry
-
-        lax.fori_loop(1, count, body, 0)
-        recv2[b, me] = send2[b, me]
-
-    for number, (low, high, tiles) in enumerate(PARTS):
-        send, recv = sends[number], recvs[number]
+                send.at[2 * place + 1 - side], far.at[place],
+                s1f.at[number, place], r1f.at[number, place], target,
+            ).wait()
 
         def wait_part(step, carry):
-            other, target = peer(step)
+            wait_far(step)
+            place, target = in_half(side, step)
             remote(
-                send.at[other], recv.at[other], s1.at[number, other], r1.at[number, other], target
+                send.at[pl.ds(2 * place, 2)], near.at[place],
+                s1n.at[number, place], r1n.at[number, place], target,
             ).wait()
             return carry
 
-        lax.fori_loop(1, count, wait_part, 0)
+        wait_far(0)
+        lax.fori_loop(1, members, wait_part, 0)
         depth = len(tiles) * LANES
-        gathered = recv[...].reshape(total, depth)
+        near_rows = near[...].reshape(members * 2 * group, depth)
+        far_rows = far[...].reshape(members * group, depth)
+        for q in range(2 * bins):
+            left, right = sides(near_picks[q], near_rows)
+            near_left[q, :, :depth] = left
+            near_right[q, :, :depth] = right
+        last = number == len(PARTS) - 1
         for b in range(bins):
-            ordered = jnp.dot(picks[b], gathered, preferred_element_type=f32)
-            turned = pltpu.roll(ordered, depth // 2, 1)
-            sign = lax.broadcasted_iota(jnp.int32, (1, depth), 1) < depth // 2
-            rotated = turned * jnp.where(sign, 1.0, -1.0)
-            by_column = jnp.swapaxes(ordered.reshape(rows, cols, own_count, depth), 0, 1)
-            by_column = by_column.reshape(channels, depth).astype(bf16)
-            for p, left in enumerate((ordered, rotated)):
-                cross = lax.dot_general(
-                    left.astype(bf16), by_column, (((1,), (1,)), ((), ())),
-                    preferred_element_type=f32,
-                )
-                if number > 0:
-                    cross = cross + totals[2 * b + p]
-                if number < len(PARTS) - 1:
-                    totals[2 * b + p] = cross
-                    continue
-                cross = cross.astype(bf16)
-                for r in range(rows):
-                    for c in range(cols):
-                        send2[b, r * cols + c, p * block : (p + 1) * block, :] = cross[
-                            r * block : (r + 1) * block, c * width : (c + 1) * width
-                        ]
-            if number == len(PARTS) - 1:
-                start_second(b)
-
-    for b in range(bins):
-
-        def wait_second(step, carry):
-            other, target = peer(step)
-            remote(
-                send2.at[b, other], recv2.at[b, other], s2.at[b, other], r2.at[b, other], target
-            ).wait()
-            return carry
-
-        lax.fori_loop(1, count, wait_second, 0)
-        depth = count * 2 * block
-        wide2[b * depth : (b + 1) * depth, :] = recv2[b].astype(f32).reshape(depth, LANES)
+            left, right = sides(far_picks[b], far_rows)
+            inward = pairs(left, near_right[side * bins + b, :, :depth])
+            outward = pairs(near_left[side * bins + b, :, :depth], right)
+            if number > 0:
+                inward = inward + in_sum[b]
+                outward = outward + out_sum[b]
+            in_sum[b] = inward
+            out_sum[b] = outward
+        if last:
+            place_units(in_sum[0], in_sum[1], store_far)
+
+            def start_far_second(step, carry):
+                place, target = in_half(1 - side, step)
+                remote(
+                    far_send.at[place], far_recv.at[member], s2f.at[place], r2f.at[member], target
+                ).start()
+                return carry
+
+            lax.fori_loop(0, members, start_far_second, 0)
+        for q in range(2 * bins):
+            cross = pairs(near_left[q, :, :depth], near_right[q, :, :depth])
+            near_sum[q] = cross + near_sum[q] if number > 0 else cross
+    place_units(near_sum[0], near_sum[1], store_near(0))
+    place_units(near_sum[2], near_sum[3], store_near(1))
+    place_units(out_sum[0], out_sum[1], store_near(2))
+
+    def start_near_second(step, carry):
+        place, target = in_half(side, step)
+        remote(
+            near_send.at[place], near_recv.at[member], s2n.at[place], r2n.at[member], target
+        ).start()
+        return carry
+
+    lax.fori_loop(1, members, start_near_second, 0)
+    near_recv[member] = near_send[member]
+
+    def wait_far_second(step, carry):
+        place, target = in_half(1 - side, step)
+        remote(
+            far_send.at[place], far_recv.at[place], s2f.at[place], r2f.at[place], target
+        ).wait()
+        return carry
+
+    def wait_near_second(step, carry):
+        place, target = in_half(side, step)
+        remote(
+            near_send.at[place], near_recv.at[place], s2n.at[place], r2n.at[place], target
+        ).wait()
+        return carry
+
+    lax.fori_loop(0, members, wait_far_second, 0)
+    depth = members * 2 * block
+    far_wide[pl.ds(pl.multiple_of((1 - side) * depth, depth), depth), :] = (
+        far_recv[...].astype(f32).reshape(depth, LANES)
+    )
+    lax.fori_loop(1, members, wait_near_second, 0)
+    far_wide[pl.ds(pl.multiple_of(side * depth, depth), depth), :] = (
+        near_recv[:, 2].astype(f32).reshape(depth, LANES)
+    )
+    near_wide[...] = near_recv[:, :2].astype(f32).reshape(2 * depth, LANES)
     fetches[5].wait()
     column = lax.broadcasted_iota(jnp.int32, (1, LANES), 1)
     for a in range(block):
-        piece = wide2[pl.ds(a, 2 * FREQS, stride=block), :].astype(bf16)
-        answer = jnp.dot(lags[...], piece, preferred_element_type=f32)[:LAGS]
+        answers = []
+        for number, wide in enumerate((near_wide, far_wide)):
+            piece = wide[pl.ds(a, FREQS, stride=block), :].astype(bf16)
+            both = jnp.dot(lags[number], piece, preferred_element_type=f32)
+            answers.append(both[:LAG_ROWS] + pltpu.roll(both[LAG_ROWS:], HALF, 1))
+        left = jnp.where(side == 0, answers[0], answers[1])
+        right = jnp.where(side == 0, answers[1], answers[0])
+        answer = jnp.where(first_lanes, left, pltpu.roll(right, HALF, 1))[:LAGS]
         same = (column // own_count == row_index) & (
             col_index * own_count + column % own_count == a
         )
@@ -376,7 +478,11 @@
     smem = pl.BlockSpec(memory_space=pltpu.SMEM)
     anywhere = pl.BlockSpec(memory_space=pltpu.HBM)
     f32, bf16 = jnp.float32, jnp.bfloat16
-    part_shapes = [(count, group, len(tiles) * LANES) for _, _, tiles in PARTS]
+    members, span_channels = count // 2, channels // 2
+    depths = [len(tiles) * LANES for _, _, tiles in PARTS]
+    part_shapes = [(count, group, depth) for depth in depths]
+    part_shapes += [(members, 2, group, depth) for depth in depths]
+    part_shapes += [(members, group, depth) for depth in depths]
     return pl.pallas_call(
         functools.partial(exchange_kernel, rows, cols),
         out_shape=jax.ShapeDtypeStruct((LAGS, block, channels // cols), f32),
@@ -392,22 +498,29 @@
             pltpu.VMEM((segment_total * own_count, LANES), f32),
             pltpu.VMEM((2, FREQS * own_count, LANES), f32),
         ]
-        + [pltpu.VMEM(shape, bf16) for shape in part_shapes + part_shapes]
+        + [pltpu.VMEM(shape, bf16) for shape in part_shapes]
         + [
             pltpu.VMEM((1, LANES), jnp.int32),
             pltpu.VMEM((count, 1, LANES), jnp.int32),
-            pltpu.VMEM((bins, channels, count * group), bf16),
-            pltpu.VMEM((2 * bins, channels, channels), f32),
-            pltpu.VMEM((bins, count, 2 * block, LANES), bf16),
-            pltpu.VMEM((bins, count, 2 * block, LANES), bf16),
-            pltpu.VMEM((2 * FREQS * block, LANES), f32),
+            pltpu.VMEM((2 * bins, span_channels, members * 2 * group), bf16),
+            pltpu.VMEM((bins, span_channels, members * group), bf16),
+            pltpu.VMEM((2 * bins, 2 * span_channels, 2 * LANES), bf16),
+            pltpu.VMEM((2 * bins, span_channels, 2 * LANES), bf16),
+            pltpu.VMEM((2 * bins, 2 * span_channels, LANES), f32),
+            pltpu.VMEM((bins, 2 * span_channels, LANES), f32),
+            pltpu.VMEM((bins, 2 * span_channels, LANES), f32),
+            pltpu.VMEM((members, 3, 2 * block, LANES), bf16),
+            pltpu.VMEM((members, 2 * block, LANES), bf16),
+            pltpu.VMEM((members, 3, 2 * block, LANES), bf16),
+            pltpu.VMEM((members, 2 * block, LANES), bf16),
+            pltpu.VMEM((FREQS * block, LANES), f32),
+            pltpu.VMEM((FREQS * block, LANES), f32),
             pltpu.VMEM((LAGS * block, LANES), f32),
-            pltpu.SemaphoreType.DMA((len(PARTS), count)),
-            pltpu.SemaphoreType.DMA((len(PARTS), count)),
-            pltpu.SemaphoreType.DMA((count,)),
-            pltpu.SemaphoreType.DMA((count,)),
-            pltpu.SemaphoreType.DMA((bins, count)),
-            pltpu.SemaphoreType.DMA((bins, count)),
+        ]
+        + [pltpu.SemaphoreType.DMA((len(PARTS), members))] * 4
+        + [pltpu.SemaphoreType.DMA((count,))] * 2
+        + [pltpu.SemaphoreType.DMA((members,))] * 4
+        + [
             pltpu.SemaphoreType.DMA((6,)),
         ],
         compiler_params=pltpu.CompilerParams(
@@ -421,7 +534,9 @@
     count = rows * cols
     fits = (
         freqs == 1
-        and FREQS % count == 0
+        and FREQS == 2 * count
+        and cols == 2
+        and rows % 2 == 0
         and traces.shape[0] == 8
         and rows * traces.shape[0] == LANES
         and FREQS // count * traces.shape[0] % 16 == 0

time: 45.5 us -> 42.1 us (0.925)
  Pallas kernels: 42.7 us -> 39.4 us
    pallas_call x1, Pallas kernels: 42.7 us -> 39.4 us  [exchange_body(): pl.pallas_call(functools.partial(exchange_kernel, rows, cols), out_shape=...]
where the time goes in v4:
time: 42.1 us; the launch traced here: 41.9 us
  Pallas kernels  39.4 us (94%)
  local copies, waits for them, and re-layouts  1.87 us (4%)
  between operations  0.66 us (2%)
    pallas_call x1, Pallas kernels, exchange_body(): pl.pallas_call(functools.partial(exchange_kernel, rows, cols), out_shape=...  39.4 us
    unnamed x1, local copies, waits for them, and re-layouts  1.87 us

profile of v4, /device:TPU:0, one launch (start us, length us, event | category | flops | bytes accessed | tf_op | source)
XLA Modules:
  0.0 41.9 jit_solution(5919512250082333268)
XLA Ops:
  0.7 39.4 %shard_map.64 = f32[65,16,128]{2,1,0:T(8,128)} custom-call(bf16[8,96000]{1,0:T(8,128)(2,1)} %traces_in.1, s32[8]{0:T(128)} %slots.1, s32[1]{0:T(128)S(6)} %copy.8.usable, bf16[384,128]{1,0:T(8,128)(2,1)} %constant.6.clone.table_in, f32[8,384]{1,0:T(8,128)} %constant.7.clone.taper_in, bf16[2,160,64]{2,1,0:T(8,128)(2,1)} %constant.8.clone.lags_in), custom_call_target="tpu_custom_call" | custom-call | tf_op jit(solution)/shard_map/pallas_call | solution.py:486
  40.0 1.9 %copy.9 = f32[65,16,128]{2,1,0:T(8,128)} copy(f32[65,16,128]{2,1,0:T(8,128)} %shard_map.64) | data formatting | bytes 1064960

commit v5 on v4

--- a/solution.py
+++ b/solution.py
@@ -136,12 +136,12 @@
 
 
 def exchange_kernel(
-    rows, cols, traces_in, slots, usable, table_in, taper_in, lags_in, out,
+    rows, cols, traces_in, slots_in, usable_in, table_in, taper_in, lags_in, out,
     traces, table, taper, lags, samples, powers, white, spectra,
     send_a, send_b, send_c, near_a, near_b, near_c, far_a, far_b, far_c, meta, recv_meta,
     near_picks, far_picks, near_left, near_right, near_sum, out_sum, in_sum,
     near_send, far_send, near_recv, far_recv, near_wide, far_wide, lagged,
-    s1n, r1n, s1f, r1f, sm, rm, s2n, r2n, s2f, r2f, own,
+    s1n, r1n, s1f, r1f, sm, rm, s2n, r2n, s2f, r2f, own, slots, usable,
 ):
     f32, bf16 = jnp.float32, jnp.bfloat16
     count = rows * cols
@@ -166,7 +166,9 @@
         )
     for number, (source, place) in enumerate(((table_in, table), (taper_in, taper), (lags_in, lags))):
         fetches.append(pltpu.make_async_copy(source, place, own.at[3 + number]))
-    for number in (4, 0, 3, 1, 2, 5):
+    fetches.append(pltpu.make_async_copy(slots_in, slots, own.at[6]))
+    fetches.append(pltpu.make_async_copy(usable_in, usable, own.at[7]))
+    for number in (4, 0, 3, 1, 2, 5, 6, 7):
         fetches[number].start()
 
     def peer(step):
@@ -194,6 +196,8 @@
             device_id=target, device_id_type=pl.DeviceIdType.MESH,
         )
 
+    fetches[6].wait()
+    fetches[7].wait()
     lane = lax.broadcasted_iota(jnp.int32, (1, LANES), 1)
     row = jnp.where(lane == own_count, usable[0], 0)
     for u in range(own_count):
@@ -256,14 +260,6 @@
         if number == 0:
             pl.semaphore_wait(barrier, count - 1)
 
-            def start_meta(step, carry):
-                other, target = peer(step)
-                remote(meta, recv_meta.at[me], sm.at[other], rm.at[me], target).start()
-                return carry
-
-            lax.fori_loop(1, count, start_meta, 0)
-            recv_meta[me] = meta[...]
-
         def start_far(step):
             place, target = in_half(1 - side, step)
             remote(
@@ -283,6 +279,15 @@
         start_far(0)
         lax.fori_loop(1, members, start_part, 0)
         near[member] = send[pl.ds(2 * member, 2)]
+        if number == 0:
+
+            def start_meta(step, carry):
+                other, target = peer(step)
+                remote(meta, recv_meta.at[me], sm.at[other], rm.at[me], target).start()
+                return carry
+
+            lax.fori_loop(1, count, start_meta, 0)
+            recv_meta[me] = meta[...]
 
     def wait_meta(step, carry):
         other, target = peer(step)
@@ -380,10 +385,15 @@
         depth = len(tiles) * LANES
         near_rows = near[...].reshape(members * 2 * group, depth)
         far_rows = far[...].reshape(members * group, depth)
-        for q in range(2 * bins):
-            left, right = sides(near_picks[q], near_rows)
-            near_left[q, :, :depth] = left
-            near_right[q, :, :depth] = right
+
+        def order_near(half):
+            for b in range(bins):
+                q = half * bins + b
+                left, right = sides(near_picks[q], near_rows)
+                near_left[q, :, :depth] = left
+                near_right[q, :, :depth] = right
+
+        order_near(side)
         last = number == len(PARTS) - 1
         for b in range(bins):
             left, right = sides(far_picks[b], far_rows)
@@ -405,6 +415,7 @@
                 return carry
 
             lax.fori_loop(0, members, start_far_second, 0)
+        order_near(1 - side)
         for q in range(2 * bins):
             cross = pairs(near_left[q, :, :depth], near_right[q, :, :depth])
             near_sum[q] = cross + near_sum[q] if number > 0 else cross
@@ -475,7 +486,6 @@
     table, taper = spectrum_table()
     lags = lag_table(segment_total, bins)
     vmem = pl.BlockSpec(memory_space=pltpu.VMEM)
-    smem = pl.BlockSpec(memory_space=pltpu.SMEM)
     anywhere = pl.BlockSpec(memory_space=pltpu.HBM)
     f32, bf16 = jnp.float32, jnp.bfloat16
     members, span_channels = count // 2, channels // 2
@@ -486,7 +496,7 @@
     return pl.pallas_call(
         functools.partial(exchange_kernel, rows, cols),
         out_shape=jax.ShapeDtypeStruct((LAGS, block, channels // cols), f32),
-        in_specs=[anywhere, smem, smem, anywhere, anywhere, anywhere],
+        in_specs=[anywhere, anywhere, anywhere, anywhere, anywhere, anywhere],
         out_specs=vmem,
         scratch_shapes=[
             pltpu.VMEM(traces.shape, bf16),
@@ -521,7 +531,9 @@
         + [pltpu.SemaphoreType.DMA((count,))] * 2
         + [pltpu.SemaphoreType.DMA((members,))] * 4
         + [
-            pltpu.SemaphoreType.DMA((6,)),
+            pltpu.SemaphoreType.DMA((8,)),
+            pltpu.SMEM(slot_channel.shape, jnp.int32),
+            pltpu.SMEM(usable_blocks.shape, jnp.int32),
         ],
         compiler_params=pltpu.CompilerParams(
             collective_id=0, has_side_effects=True, vmem_limit_bytes=60 * 1024 * 1024

time: 42.1 us -> 41.3 us (0.981)
  Pallas kernels: 39.4 us -> 38.6 us
    pallas_call x1, Pallas kernels: 39.4 us -> 38.6 us  [exchange_body(): pl.pallas_call(functools.partial(exchange_kernel, rows, cols), out_shape=...]
where the time goes in v5:
time: 41.3 us; the launch traced here: 41.1 us
  Pallas kernels  38.6 us (93%)
  local copies, waits for them, and re-layouts  1.87 us (5%)
  between operations  0.66 us (2%)
    pallas_call x1, Pallas kernels, exchange_body(): pl.pallas_call(functools.partial(exchange_kernel, rows, cols), out_shape=...  38.6 us
    unnamed x1, local copies, waits for them, and re-layouts  1.87 us

profile of v5, /device:TPU:0, one launch (start us, length us, event | category | flops | bytes accessed | tf_op | source)
XLA Modules:
  0.0 41.1 jit_solution(2471838009029815321)
XLA Ops:
  0.7 38.6 %shard_map.64 = f32[65,16,128]{2,1,0:T(8,128)} custom-call(bf16[8,96000]{1,0:T(8,128)(2,1)} %traces_in.1, s32[8]{0:T(128)} %slots_in.1, s32[1]{0:T(128)S(6)} %copy.8.usable_in, bf16[384,128]{1,0:T(8,128)(2,1)} %constant.6.clone.table_in, f32[8,384]{1,0:T(8,128)} %constant.7.clone.taper_in, bf16[2,160,64]{2,1,0:T(8,128)(2,1)} %constant.8.clone.lags_in), custom_call_target="tpu_custom_call" | custom-call | tf_op jit(solution)/shard_map/pallas_call | solution.py:496
  39.3 1.9 %copy.9 = f32[65,16,128]{2,1,0:T(8,128)} copy(f32[65,16,128]{2,1,0:T(8,128)} %shard_map.64) | data formatting | bytes 1064960

commit v6 on v5

--- a/solution.py
+++ b/solution.py
@@ -188,7 +188,7 @@
         )
         return carry
 
-    lax.fori_loop(1, count, greet, 0)
+    lax.fori_loop(1, count, greet, 0, unroll=True)
 
     def remote(src, dst, send_sem, recv_sem, target):
         return pltpu.make_async_remote_copy(
@@ -277,7 +277,7 @@
             return carry
 
         start_far(0)
-        lax.fori_loop(1, members, start_part, 0)
+        lax.fori_loop(1, members, start_part, 0, unroll=True)
         near[member] = send[pl.ds(2 * member, 2)]
         if number == 0:
 
@@ -286,7 +286,7 @@
                 remote(meta, recv_meta.at[me], sm.at[other], rm.at[me], target).start()
                 return carry
 
-            lax.fori_loop(1, count, start_meta, 0)
+            lax.fori_loop(1, count, start_meta, 0, unroll=True)
             recv_meta[me] = meta[...]
 
     def wait_meta(step, carry):
@@ -294,7 +294,7 @@
         remote(meta, recv_meta.at[other], sm.at[other], rm.at[other], target).wait()
         return carry
 
-    lax.fori_loop(1, count, wait_meta, 0)
+    lax.fori_loop(1, count, wait_meta, 0, unroll=True)
     known = recv_meta[...].reshape(count, LANES).astype(f32).astype(bf16)
 
     def choose(half, pieces, picks):
@@ -381,7 +381,7 @@
             return carry
 
         wait_far(0)
-        lax.fori_loop(1, members, wait_part, 0)
+        lax.fori_loop(1, members, wait_part, 0, unroll=True)
         depth = len(tiles) * LANES
         near_rows = near[...].reshape(members * 2 * group, depth)
         far_rows = far[...].reshape(members * group, depth)
@@ -414,7 +414,7 @@
                 ).start()
                 return carry
 
-            lax.fori_loop(0, members, start_far_second, 0)
+            lax.fori_loop(0, members, start_far_second, 0, unroll=True)
         order_near(1 - side)
         for q in range(2 * bins):
             cross = pairs(near_left[q, :, :depth], near_right[q, :, :depth])
@@ -430,7 +430,7 @@
         ).start()
         return carry
 
-    lax.fori_loop(1, members, start_near_second, 0)
+    lax.fori_loop(1, members, start_near_second, 0, unroll=True)
     near_recv[member] = near_send[member]
 
     def wait_far_second(step, carry):
@@ -447,12 +447,12 @@
         ).wait()
         return carry
 
-    lax.fori_loop(0, members, wait_far_second, 0)
+    lax.fori_loop(0, members, wait_far_second, 0, unroll=True)
     depth = members * 2 * block
     far_wide[pl.ds(pl.multiple_of((1 - side) * depth, depth), depth), :] = (
         far_recv[...].astype(f32).reshape(depth, LANES)
     )
-    lax.fori_loop(1, members, wait_near_second, 0)
+    lax.fori_loop(1, members, wait_near_second, 0, unroll=True)
     far_wide[pl.ds(pl.multiple_of(side * depth, depth), depth), :] = (
         near_recv[:, 2].astype(f32).reshape(depth, LANES)
     )

time: 41.3 us -> 41.1 us (level)
  no operation moved by 1% of the time
where the time goes in v6:
time: 41.1 us; the launch traced here: 40.9 us
  Pallas kernels  38.4 us (93%)
  local copies, waits for them, and re-layouts  1.87 us (5%)
  between operations  0.66 us (2%)
    pallas_call x1, Pallas kernels, exchange_body(): pl.pallas_call(functools.partial(exchange_kernel, rows, cols), out_shape=...  38.4 us
    unnamed x1, local copies, waits for them, and re-layouts  1.87 us

profile of v6, /device:TPU:0, one launch (start us, length us, event | category | flops | bytes accessed | tf_op | source)
XLA Modules:
  0.0 40.9 jit_solution(3438927100931920436)
XLA Ops:
  0.7 38.4 %shard_map.64 = f32[65,16,128]{2,1,0:T(8,128)} custom-call(bf16[8,96000]{1,0:T(8,128)(2,1)} %traces_in.1, s32[8]{0:T(128)} %slots_in.1, s32[1]{0:T(128)S(6)} %copy.8.usable_in, bf16[384,128]{1,0:T(8,128)(2,1)} %constant.6.clone.table_in, f32[8,384]{1,0:T(8,128)} %constant.7.clone.taper_in, bf16[2,160,64]{2,1,0:T(8,128)(2,1)} %constant.8.clone.lags_in), custom_call_target="tpu_custom_call" | custom-call | tf_op jit(solution)/shard_map/pallas_call | solution.py:496
  39.0 1.9 %copy.9 = f32[65,16,128]{2,1,0:T(8,128)} copy(f32[65,16,128]{2,1,0:T(8,128)} %shard_map.64) | data formatting | bytes 1064960
